TPU v7x, 512 devices: a whole 4x8x8 slice. The times are simulated.
512 devices in a mesh: row: 16 (over z_hi, y), col: 32 (over x, z_lo, core).
Axes of the slice: x: 4, y: 8, z: 8 (z_hi: 2, z_lo: 4; z = z_hi * 4 + z_lo), core: 2. Of those that a mesh axis runs over, the one named last changes fastest.
Arguments:
- amplitudes: float32 [6, 16, 128, 2048], P(None, None, 'col', 'row'), may hold values from -0.054 to 0.054
- integrals: float32 [12, 16, 128, 2048], P(None, None, 'col', 'row'), may hold values from -6 to 6
- occupied_left: float32 [6], replicated, may hold values from -2 to -0.5
- occupied_right: float32 [12], replicated, may hold values from -2 to -0.5
- virtual_energy: float32 [2048], replicated, may hold values from 0.5 to 3
Outputs:
- update: float32 [6, 12, 16, 128, 2048], P(None, None, None, 'col', 'row')
All inputs are finite; a program needn't handle non-finite values.
Results may differ from a plain program's by a relative error of at most 0.00007.
Values sent between devices are 32-bit elements; how exact they have to be, the bound alone decides.
A program may use at most 192 MiB of HBM per device.

v0:
```python
import jax
import jax.numpy as jnp
from jax import lax
from jax.sharding import PartitionSpec as P


def body(amplitudes, integrals, occupied_left, occupied_right, virtual_energy):
    col_count = lax.axis_size("col")
    left_count, lead_count, sub_count, local_width = amplitudes.shape
    full_width = lead_count * local_width

    def arrange(stored):
        number = stored.shape[0]
        digits = stored.reshape(number, lead_count, sub_count, col_count, sub_count)
        digits = jnp.transpose(digits, (0, 1, 4, 3, 2))
        return digits.reshape(number, lead_count, 1, sub_count, col_count, 1, sub_count)

    amp_moved, int_moved = (
        lax.all_to_all(
            lax.all_to_all(arrange(amplitudes), "row", split_axis=1, concat_axis=2, tiled=True),
            "col",
            split_axis=4,
            concat_axis=5,
            tiled=True,
        ),
        lax.all_to_all(
            lax.all_to_all(arrange(integrals), "row", split_axis=1, concat_axis=2, tiled=True),
            "col",
            split_axis=4,
            concat_axis=5,
            tiled=True,
        ),
    )
    tilde = 2.0 * amplitudes - amp_moved.reshape(amplitudes.shape)
    lmat = 2.0 * integrals - int_moved.reshape(integrals.shape)
    highest = lax.Precision.HIGHEST
    tilde_all = lax.all_gather(tilde, "col", axis=2, tiled=True).reshape(
        left_count, full_width, local_width
    )
    cycle = jnp.einsum(
        "ica,jxyc->ijxya",
        tilde_all,
        lax.all_gather(lmat, "row", axis=3, tiled=True),
        precision=highest,
    )
    energy_a = lax.dynamic_slice_in_dim(
        virtual_energy, lax.axis_index("row") * local_width, local_width, 0
    )
    energy_b = lax.dynamic_slice_in_dim(
        virtual_energy.reshape(lead_count, local_width),
        lax.axis_index("col") * sub_count,
        sub_count,
        1,
    )
    denom = energy_a[None, None, None, None, :] + energy_b[None, None, :, :, None]
    denom = (
        denom - occupied_left[:, None, None, None, None] - occupied_right[None, :, None, None, None]
    )
    return cycle / denom


def solution(mesh):
    return jax.shard_map(
        body,
        mesh=mesh,
        in_specs=(P(None, None, "col", "row"), P(None, None, "col", "row"), P(), P(), P()),
        out_specs=P(None, None, None, "col", "row"),
        check_vma=False,
    )
```

profile of v0, /device:TPU:1, one launch (start us, length us, event | category | flops | bytes accessed | tf_op | source)
XLA Modules:
  0.0 340.0 jit_solution(6239595066212941624)
XLA Ops:
  6.5 1.4 copy.57
  7.9 0.8 copy.58
  8.7 0.5 reshape.64
  9.3 27.9 %all_to_all.42 = f32[16,1,3072]{2,1,0:T(1,128)S(1)} all-to-all(f32[16,1,3072]{2,1,0:T(1,128)S(1)} %reshape.64), channel_id=1, replica_groups=mesh['row'=16,'col'=32] {'row'}, dimensions={0} | all-to-all | bytes 393216 | tf_op jit(solution)/shard_map/all_to_all | solution.py:20
  37.2 0.5 broadcast.28
  37.7 1.0 reduce
  39.2 1.2 copy.59
  40.4 1.2 reshape.66
  41.6 18.8 %all_to_all.43 = f32[32,1,1536]{2,1,0:T(1,128)S(1)} all-to-all(f32[32,1,1536]{2,1,0:T(1,128)S(1)} %reshape.66), channel_id=1, replica_groups=mesh['row'=16,'col'=32] {'col'}, dimensions={0} | all-to-all | bytes 393216 | tf_op jit(solution)/shard_map/all_to_all | solution.py:19
  60.4 1.0 reduce.1
  61.5 1.1 reshape.67
  63.5 1.7 fusion.5
  65.2 1.0 copy.51
  66.2 2.6 copy.52
  68.8 2.4 reshape.68
  71.2 19.3 %all_to_all.44 = f32[16,1,6144]{2,1,0:T(1,128)S(1)} all-to-all(f32[16,1,6144]{2,1,0:T(1,128)S(1)} %reshape.68), channel_id=1, replica_groups=mesh['row'=16,'col'=32] {'row'}, dimensions={0} | all-to-all | bytes 786432 | tf_op jit(solution)/shard_map/all_to_all | solution.py:27
  90.5 1.5 reduce.2
  92.0 0.8 reshape.69
  92.8 1.5 bitcast_bitcast_fusion
  94.3 4.3 %copy.53 = f32[12,1,16,4,32,1,4]{2,3,6,0,5,1,4:T(4,128)S(1)} copy(f32[12,1,16,4,32,1,4]{4,6,3,0,2,5,1:T(4,128)} %bitcast_bitcast_fusion) | data formatting | bytes 786432 | tf_op jit(solution)/shard_map/all_to_all | solution.py:27
  98.6 3.1 reshape.70
  101.7 23.0 %all_to_all.45 = f32[32,1,3072]{2,1,0:T(1,128)S(1)} all-to-all(f32[32,1,3072]{2,1,0:T(1,128)} %reshape.70), channel_id=1, replica_groups=mesh['row'=16,'col'=32] {'col'}, dimensions={0} | all-to-all | bytes 786432 | tf_op jit(solution)/shard_map/all_to_all | solution.py:26
  124.7 2.3 reduce.3
  127.0 3.4 reshape.71
  130.4 2.5 copy.54
  132.9 2.3 copy.55
  135.2 0.8 fusion.4
  136.5 1.0 all-gather.5.cloned.1.call-done
  137.6 7.4 %copy.62 = f32[6,16,128,128]{3,2,1,0:T(8,128)} copy(f32[6,16,128,128]{3,1,2,0:T(8,128)} %all-gather.5.cloned.1.call-done) | data formatting | bytes 12582912 | tf_op jit(solution)/shard_map/all_gather | solution.py:37
  144.9 166.3 %all-gather.3.cloned.1.call-done = f32[12,16,4,2048]{3,1,2,0:T(8,128)} async-done(((f32[12,16,4,128]{3,1,2,0:T(8,128)}), f32[12,16,4,2048]{3,1,2,0:T(8,128)}) %all-gather.3.cloned.1.call-update) | async-done | bytes 6291472 | tf_op jit(solution)/shard_map/all_gather | solution.py:43
  311.2 19.0 %bitcast_divide_fusion = f32[6,12,16,4,128]{4,2,0,3,1:T(8,128)S(1)} fusion(f32[6,2048,128,1,1]{2,1,0,4,3:T(8,128)} %bitcast.46, f32[12,16,4,2048]{3,1,2,0:T(8,128)} %all-gather.3.cloned.1.call-done, f32[12]{0:T(128)S(1)} %copy-done.3, f32[6,16,4,128]{3,1,0,2:T(8,128)S(1)} %broadcast_subtract_fusion), kind=kOutput, calls=%fused_computation.2 | convolution fusion | flops 14496694272 | bytes 15138864 | tf_op jit(solution)/shard_map/ica,jxyc->ijxya/dot_general | solution.py:40
  330.2 2.9 copy.64
  (21 shorter events, 1.8 us)
Async XLA Ops:
  6.5 131.0 %all-gather.5.cloned.1.call-start = ((), (), s32[]{:S(2)}) async-start(), calls=%async_computation.5 | async-start | bytes 6488064 | tf_op jit(solution)/shard_map/all_gather | solution.py:37
  62.6 2.6 copy-start
  65.1 246.0 %all-gather.3.cloned.1.call-start = ((), (), s32[]{:S(2)}) async-start(), calls=%async_computation.4 | async-start | bytes 6684672 | tf_op jit(solution)/shard_map/all_gather | solution.py:43
  132.9 3.2 copy-start.1
  132.9 3.5 %copy-start.2 = (f32[6]{0:T(128)S(1)}, f32[6]{0:T(128)}, u32[]{:S(2)}) copy-start(f32[6]{0:T(128)} %param.7) | copy-start | bytes 76
  136.5 174.7 %copy-start.3 = (f32[12]{0:T(128)S(1)}, f32[12]{0:T(128)}, u32[]{:S(2)}) copy-start(f32[12]{0:T(128)} %param.8) | copy-start | bytes 148
Sparse Core Ops, SparseCore 0:
  65.3 72.2 all-gather.4
  140.6 170.5 all-gather.2
where the time goes:
time: 345 us; the launch traced here: 340 us
  waiting for transfers between devices  167 us (48%)
  blocking collectives  89 us (26%)
  local copies, waits for them, and re-layouts  42.5 us (12%)
  matrix products  19 us (6%)
  between operations  13.6 us (4%)
  other arithmetic  8.49 us (2%)
    all_gather x1, waiting for transfers between devices, body(): lax.all_gather(lmat, 'row', axis=3, tiled=True)  166 us
    all_to_all x1, blocking collectives, body(): lax.all_to_all(arrange(amplitudes), 'row', split_axis=1, concat_axis=2, t...  27.9 us
    all_to_all x1, blocking collectives, body(): lax.all_to_all(lax.all_to_all(arrange(integrals), 'row', split_axis=1, co...  23 us
    all_to_all x1, blocking collectives, body(): lax.all_to_all(arrange(integrals), 'row', split_axis=1, concat_axis=2, ti...  19.3 us
    dot_general x1, matrix products, body(): jnp.einsum('ica,jxyc->ijxya', tilde_all, lax.all_gather(lmat, 'row', axis...  19 us
    all_to_all x1, blocking collectives, body(): lax.all_to_all(lax.all_to_all(arrange(amplitudes), 'row', split_axis=1, c...  18.8 us
    unnamed x18, local copies, waits for them, and re-layouts  15.3 us
    all_gather x1, local copies, waits for them, and re-layouts, body(): lax.all_gather(tilde, 'col', axis=2, tiled=True)  7.35 us
  transfers between devices with their start and end apart: 2, of which 2 were waited for; matrix products, arithmetic and copies ran while one was open for 11% of the time, Pallas kernels for 0%

commit v1 on v0

v1 whole, which is shorter than its diff:
```python
import functools
import heapq

import jax
import jax.numpy as jnp
from jax import lax
from jax.experimental import pallas as pl
from jax.experimental.pallas import tpu as pltpu
from jax.sharding import PartitionSpec as P

MESH = pl.DeviceIdType.MESH
LANES = 128
F32 = jnp.float32
BF16 = jnp.bfloat16

ROW_DIMS = (2, 8)
COL_DIMS = (4, 4, 2)
GROUPS = 2


class Links:
    def __init__(self):
        self.free = {}

    def send(self, link, now, size):
        start = max(now, self.free.get(link, 0.0))
        self.free[link] = start + size
        return start + size + 1.0


def split(x):
    high = x.astype(BF16)
    return high, (x - high.astype(F32)).astype(BF16)


def load_tile(ref, b):
    return ref.reshape(-1, LANES, LANES)[b]


def store_tile(ref, b, value):
    ref.reshape(-1, LANES, LANES)[b] = value


def swap_low_digits(x, digit):
    rows = lax.broadcasted_iota(jnp.int32, x.shape, 0)
    lanes = lax.broadcasted_iota(jnp.int32, x.shape, 1)
    bit = 1
    while bit < digit:
        row_bit, lane_bit = rows & bit, lanes & bit
        upper = pltpu.roll(pltpu.roll(x, x.shape[0] - bit, 0), bit, 1)
        lower = pltpu.roll(pltpu.roll(x, bit, 0), x.shape[1] - bit, 1)
        x = jnp.where(row_bit == lane_bit, x, jnp.where(lane_bit == bit, upper, lower))
        bit *= 2
    return x


def kernel(
    left_count,
    right_count,
    int_hbm,
    amp_hbm,
    occ_left,
    occ_right,
    energy,
    out_hbm,
    int_own,
    amp_own,
    int_row,
    amp_row,
    int_send,
    amp_send,
    int_col,
    amp_col,
    lm,
    tl,
    lhs,
    rhs,
    acc,
    recip,
    base,
    staged,
    own_sem,
    keep_sem,
    row_send,
    row_recv,
    col_send,
    col_recv,
    lm_send,
    lm_recv,
    tl_send,
    tl_recv,
    out_sem,
):
    halves, ring = ROW_DIMS
    xs, runs, cores = COL_DIMS
    rows, cols = halves * ring, xs * runs * cores
    sub = LANES // cols
    cells = rows * sub
    r, s = lax.axis_index("row"), lax.axis_index("col")
    half, y = r // ring, r % ring
    x, run, core = s // (runs * cores), (s // cores) % runs, s % cores
    per_group = right_count // GROUPS
    group_rows = per_group * cells
    blocks = group_rows // LANES
    amp_blocks = left_count * cells // LANES

    def row_of(a, b):
        return a * ring + b

    def col_of(a, b, c):
        return (a * runs + b) * cores + c

    def remote(src, dst, send_sem, recv_sem, device):
        return pltpu.make_async_remote_copy(
            src_ref=src,
            dst_ref=dst,
            send_sem=send_sem,
            recv_sem=recv_sem,
            device_id=device,
            device_id_type=MESH,
        )

    own_copies = [
        pltpu.make_async_copy(int_hbm, int_own, own_sem.at[0]),
        pltpu.make_async_copy(amp_hbm, amp_own, own_sem.at[1]),
    ]
    for copy in own_copies:
        copy.start()

    barrier = pltpu.get_barrier_semaphore()

    def greet_row(k, carry):
        pl.semaphore_signal(barrier, inc=1, device_id=((r + k) % rows, s), device_id_type=MESH)
        return carry

    def greet_col(k, carry):
        pl.semaphore_signal(barrier, inc=1, device_id=(r, (s + k) % cols), device_id_type=MESH)
        return carry

    lax.fori_loop(1, rows, greet_row, 0)
    lax.fori_loop(1, cols, greet_col, 0)
    pl.semaphore_wait(barrier, rows - 1 + cols - 1)

    parts = []
    for g in range(GROUPS):
        numbers = pl.ds(g * per_group, per_group)
        slabs = pl.ds(g * blocks, blocks)
        parts.append((int_hbm, int_row, int_send, int_col, numbers, slabs, g * blocks, blocks))
    everything = pl.ds(0, left_count)
    parts.append(
        (amp_hbm, amp_row, amp_send, amp_col, everything, pl.ds(0, amp_blocks), 0, amp_blocks)
    )

    keeps = []
    for n, (source, landed, _, _, numbers, _, _, _) in enumerate(parts):

        def send_row(k, carry, n=n, source=source, landed=landed, numbers=numbers):
            to = (r + k) % rows
            remote(
                source.at[numbers, to],
                landed.at[numbers, r],
                row_send.at[n],
                row_recv.at[n],
                (to, s),
            ).start()
            return carry

        lax.fori_loop(1, rows, send_row, 0)
        keep = pltpu.make_async_copy(source.at[numbers, r], landed.at[numbers, r], keep_sem.at[n])
        keep.start()
        keeps.append(keep)

    own_energy = energy[pl.ds(r, 1), :]
    lane = lax.broadcasted_iota(jnp.int32, (sub, LANES), 1)
    wanted = lax.broadcasted_iota(jnp.int32, (sub, LANES), 0) + sub * s
    for u in range(rows):
        spread = jnp.broadcast_to(energy[u : u + 1, :], (sub, LANES))
        chosen = jnp.sum(jnp.where(lane == wanted, spread, 0.0), axis=1, keepdims=True)
        base[u] = own_energy + chosen
    both_energies = base[...].reshape(cells, LANES)

    def reciprocals(j, carry):
        for i in range(left_count):
            recip[i, j] = 1.0 / (both_energies - occ_left[i] - occ_right[j])
        return carry

    lax.fori_loop(0, right_count, reciprocals, 0)

    def row_part(n):
        source, landed, turned, arrived, numbers, slabs, first, count = parts[n]
        if rows > 1:
            whole = landed.at[numbers, pl.ds(0, rows - 1)]
            both = remote(whole, whole, row_send.at[n], row_recv.at[n], (r, (s + 1) % cols))
            both.wait_recv()
        keeps[n].wait()
        for b in range(first, first + count):
            store_tile(turned, b, load_tile(landed, b).T)

        def send_col(k, carry):
            to = (s + k) % cols
            remote(
                turned.at[slabs, to],
                arrived.at[slabs, s],
                col_send.at[n],
                col_recv.at[n],
                (r, to),
            ).start()
            return carry

        lax.fori_loop(1, cols, send_col, 0)
        for b in range(first, first + count):
            arrived[b, s] = turned[b, s]

    def col_part(n):
        source, landed, turned, arrived, numbers, slabs, first, count = parts[n]
        whole = arrived.at[slabs, pl.ds(0, cols - 1)]
        remote(whole, whole, col_send.at[n], col_recv.at[n], (r, (s + 1) % cols)).wait_recv()
        own, into = (int_own, lm.at[r]) if n < GROUPS else (amp_own, tl.at[s])
        for b in range(first, first + count):
            moved = swap_low_digits(load_tile(arrived, b).T, sub)
            store_tile(into, b, 2.0 * load_tile(own, b) - moved)

    def finish_sends(n):
        source, landed, turned, arrived, numbers, slabs, first, count = parts[n]
        if rows > 1:
            whole = landed.at[numbers, pl.ds(0, rows - 1)]
            remote(whole, whole, row_send.at[n], row_recv.at[n], (r, (s + 1) % cols)).wait_send()
        whole = arrived.at[slabs, pl.ds(0, cols - 1)]
        remote(whole, whole, col_send.at[n], col_recv.at[n], (r, (s + 1) % cols)).wait_send()

    sends = []
    count_of = {"lm": 0, "tl": 0}
    links = Links()
    heap = []
    serial = [0]

    def at(time, act):
        serial[0] += 1
        heapq.heappush(heap, (time, serial[0], act))

    def lm_chunk(slot, g):
        return lm.at[slot, pl.ds(g * group_rows, group_rows)]

    def send_lm(slot, g, device):
        chunk = lm_chunk(slot, g)
        copy = remote(chunk, chunk, lm_send.at[count_of["lm"]], lm_recv.at[slot, g], device)
        count_of["lm"] += 1
        copy.start()
        sends.append(copy)

    def await_lm(slot, g):
        chunk = lm_chunk(slot, g)
        remote(chunk, chunk, lm_send.at[0], lm_recv.at[slot, g], (r, (s + 1) % cols)).wait_recv()

    def send_tl(slot, device):
        chunk = tl.at[slot]
        copy = remote(chunk, chunk, tl_send.at[count_of["tl"]], tl_recv.at[slot], device)
        count_of["tl"] += 1
        copy.start()
        sends.append(copy)

    def await_tl(slot):
        chunk = tl.at[slot]
        remote(chunk, chunk, tl_send.at[0], tl_recv.at[slot], (r, (s + 1) % cols)).wait_recv()

    lm_ready, tl_ready = {}, []
    far_y, far_x = ring // 2, xs // 2
    lm_time = group_rows * LANES * 4 * 2 / 100e3
    tl_time = left_count * cells * LANES * 4 * 2 / 100e3

    def ways(distance, far, parity):
        if distance + 1 < far:
            return (1, -1)
        return ((1,) if parity else (-1,)) if distance + 1 == far else ()

    def spread_lm(now, z, g, distance, came):
        place = half if z == 0 else (half + z) % halves
        slot = row_of(place, (y - came * distance) % ring)
        if distance:
            await_lm(slot, g)
        elif z:
            await_lm(slot, g)
        lm_ready.setdefault(came * distance % ring, []).append(now)
        for way in ways(distance, far_y, (z + g) % 2):
            if distance == 0 or way == came:
                send_lm(slot, g, (row_of(half, (y + way) % ring), s))
                then = links.send(("y", way), now, lm_time)
                at(then, functools.partial(spread_lm, then, z, g, distance + 1, way))
        if z == 0 and distance == 0:
            for k in range(1, halves):
                send_lm(slot, g, (row_of((half + k) % halves, y), s))
                then = links.send("half", now, 2 * lm_time)
                at(then, functools.partial(spread_lm, then, k, g, 0, 1))
        compute(now)

    def spread_tl(now, k, distance, came, first):
        slot = col_of((x - came * distance) % xs, (run - k) % runs, core)
        if not first:
            await_tl(slot)
        tl_ready.append(now)
        for way in ways(distance, far_x, k % 2):
            if distance == 0 or way == came:
                send_tl(slot, (r, col_of((x + way) % xs, run, core)))
                then = links.send(("x", way), now, tl_time)
                at(then, functools.partial(spread_tl, then, k, distance + 1, way, False))
        if first:
            for other in range(1, runs):
                send_tl(slot, (r, col_of(x, (run + other) % runs, core)))
                then = links.send("run", now, tl_time)
                at(then, functools.partial(spread_tl, then, other, 0, 1, False))
        if cores > 1:
            send_tl(slot, (r, col_of(x, run, 1 - core)))
            then = links.send("core", now, tl_time / 6)
            at(then, functools.partial(sibling, then, k, distance, came))
        compute(now)

    def sibling(now, k, distance, came):
        await_tl(col_of((x - came * distance) % xs, (run - k) % runs, 1 - core))
        tl_ready.append(now)
        compute(now)

    def start_lm(now, g):
        col_part(g)
        spread_lm(now, 0, g, 0, 1)

    def start_tl(now):
        col_part(GROUPS)
        spread_tl(now, 0, 0, 1, True)

    done = set()

    def compute(now):
        if len(tl_ready) < cols:
            return
        for place, times in list(lm_ready.items()):
            if len(times) == halves * GROUPS and place not in done:
                products(place, not done)
                done.add(place)

    def products(place, first):
        at_y = (y - place) % ring
        width = halves * LANES
        for z in range(halves):
            slot = row_of(z, at_y)

            def left(b, carry, z=z, slot=slot):
                here = pl.ds(pl.multiple_of(b * LANES, LANES), LANES)
                high, low = split(lm[slot, here, :])
                lhs[here, z * LANES : (z + 1) * LANES] = high
                lhs[here, width + z * LANES : width + (z + 1) * LANES] = low
                lhs[here, 2 * width + z * LANES : 2 * width + (z + 1) * LANES] = high
                return carry

            lax.fori_loop(0, right_count * cells // LANES, left, 0)
            for i in range(left_count):
                high, low = split(tl[:, i, slot].reshape(LANES, LANES))
                across = slice(i * LANES, (i + 1) * LANES)
                rhs[z * LANES : (z + 1) * LANES, across] = high
                rhs[width + z * LANES : width + (z + 1) * LANES, across] = high
                rhs[2 * width + z * LANES : 2 * width + (z + 1) * LANES, across] = low
        tile = 256

        def multiply(m, carry):
            here = pl.ds(pl.multiple_of(m * tile, tile), tile)
            for n in range(left_count * LANES // tile):
                across = slice(n * tile, (n + 1) * tile)
                product = jnp.dot(lhs[here, :], rhs[:, across], preferred_element_type=F32)
                acc[here, across] = product if first else acc[here, across] + product
            return carry

        lax.fori_loop(0, right_count * cells // tile, multiply, 0)

    def turn(n):
        return lambda: row_part(n)

    for n in range(GROUPS + 1):
        at(4.0 + n, turn(n))
    for g in range(GROUPS):
        at(10.0 + 2.0 * g, functools.partial(start_lm, 10.0 + 2.0 * g, g))
    start = 10.0 + 2.0 * GROUPS
    at(start, functools.partial(start_tl, start))
    for copy in own_copies:
        at(9.0, copy.wait)
    while heap:
        heapq.heappop(heap)[2]()
    assert len(done) == ring

    def finish(j, carry):
        here = pl.ds(pl.multiple_of(j * cells, cells), cells)
        for i in range(left_count):
            result = acc[here, i * LANES : (i + 1) * LANES] * recip[i, j]
            staged[i, j] = result.reshape(rows, sub, LANES)
        pltpu.make_async_copy(staged.at[:, j], out_hbm.at[:, j], out_sem.at[j]).start()
        return carry

    lax.fori_loop(0, right_count, finish, 0)
    for n in range(GROUPS + 1):
        finish_sends(n)
    for copy in sends:
        copy.wait_send()

    def written(j, carry):
        pltpu.make_async_copy(staged.at[:, j], out_hbm.at[:, j], out_sem.at[j]).wait()
        return carry

    lax.fori_loop(0, right_count, written, 0)


def body(amplitudes, integrals, occupied_left, occupied_right, virtual_energy):
    left_count, rows, sub, width = amplitudes.shape
    right_count = integrals.shape[0]
    cols = width // sub
    cells = rows * sub
    amp_blocks, int_blocks = left_count * cells // LANES, right_count * cells // LANES
    depth = 3 * ROW_DIMS[0] * LANES
    dma = pltpu.SemaphoreType.DMA
    anywhere = pl.BlockSpec(memory_space=pl.ANY)
    scalars = pl.BlockSpec(memory_space=pltpu.SMEM)
    return pl.pallas_call(
        functools.partial(kernel, left_count, right_count),
        out_shape=jax.ShapeDtypeStruct((left_count, right_count, rows, sub, width), F32),
        in_specs=[
            anywhere,
            anywhere,
            scalars,
            scalars,
            pl.BlockSpec(memory_space=pltpu.VMEM),
        ],
        out_specs=anywhere,
        scratch_shapes=[
            pltpu.VMEM(integrals.shape, F32),
            pltpu.VMEM(amplitudes.shape, F32),
            pltpu.VMEM(integrals.shape, F32),
            pltpu.VMEM(amplitudes.shape, F32),
            pltpu.VMEM((int_blocks, cols, sub, LANES), F32),
            pltpu.VMEM((amp_blocks, cols, sub, LANES), F32),
            pltpu.VMEM((int_blocks, cols, sub, LANES), F32),
            pltpu.VMEM((amp_blocks, cols, sub, LANES), F32),
            pltpu.VMEM((rows, right_count * cells, LANES), F32),
            pltpu.VMEM((cols,) + amplitudes.shape, F32),
            pltpu.VMEM((right_count * cells, depth), BF16),
            pltpu.VMEM((depth, left_count * LANES), BF16),
            pltpu.VMEM((right_count * cells, left_count * LANES), F32),
            pltpu.VMEM((left_count, right_count, cells, LANES), F32),
            pltpu.VMEM((rows, sub, LANES), F32),
            pltpu.VMEM((left_count, right_count, rows, sub, LANES), F32),
            dma((2,)),
            dma((GROUPS + 1,)),
            dma((GROUPS + 1,)),
            dma((GROUPS + 1,)),
            dma((GROUPS + 1,)),
            dma((GROUPS + 1,)),
            dma((16 * GROUPS,)),
            dma((rows, GROUPS)),
            dma((40,)),
            dma((cols,)),
            dma((right_count,)),
        ],
        compiler_params=pltpu.CompilerParams(
            collective_id=0, has_side_effects=True, vmem_limit_bytes=60 * 1024 * 1024
        ),
    )(
        integrals,
        amplitudes,
        occupied_left,
        occupied_right,
        virtual_energy.reshape(rows, width),
    )


def solution(mesh):
    return jax.shard_map(
        body,
        mesh=mesh,
        in_specs=(P(None, None, "col", "row"), P(None, None, "col", "row"), P(), P(), P()),
        out_specs=P(None, None, None, "col", "row"),
        check_vma=False,
    )
```

time: 345 us -> 143 us (0.41)
  the two profiles are of different devices: /device:TPU:1 before, /device:TPU:177 now
where the time goes in v1:
time: 143 us
  Pallas kernels  139 us (97%)
  local copies, waits for them, and re-layouts  3.36 us (2%)
    pallas_call x1, Pallas kernels, body(): pl.pallas_call(functools.partial(kernel, left_count, right_count), out_sh...  139 us
    unnamed x1, local copies, waits for them, and re-layouts  3.36 us

profile of v1, /device:TPU:177, one launch (start us, length us, event | category | flops | bytes accessed | tf_op | source)
XLA Modules:
  0.0 142.8 jit_solution(18439387232395605223)
XLA Ops:
  0.0 139.4 %shard_map.55 = f32[6,12,16,4,128]{4,3,2,1,0:T(4,128)} custom-call(f32[12,16,4,128]{3,2,1,0:T(4,128)} %int_hbm.1, f32[6,16,4,128]{3,2,1,0:T(4,128)} %amp_hbm.1, f32[6]{0:T(128)} %occ_left.1, f32[12]{0:T(128)} %occ_right.1, f32[16,128]{1,0:T(8,128)} %bitcast.1), custom_call_target="tpu_custom_call" | custom-call | tf_op jit(solution)/shard_map/pallas_call | solution.py:419
  139.4 3.4 %copy.7 = f32[6,12,16,4,128]{4,3,2,1,0:T(4,128)} copy(f32[6,12,16,4,128]{4,3,2,1,0:T(4,128)} %shard_map.55) | data formatting | bytes 4718592

commit v2 on v1

v2 whole, which is shorter than its diff:
```python
import functools
import heapq

import jax
import jax.numpy as jnp
from jax import lax
from jax.experimental import pallas as pl
from jax.experimental.pallas import tpu as pltpu
from jax.sharding import PartitionSpec as P

MESH = pl.DeviceIdType.MESH
LANES = 128
F32 = jnp.float32
BF16 = jnp.bfloat16

ROW_DIMS = (2, 8)
COL_DIMS = (4, 4, 2)
GROUPS = 3
AMP_TURN = 1
RING_SENT = (0.0, 0.0, 0.0, 0.0)
RING_DONE = (4.5, 7.0, 9.5, 12.5)
PLANE_DONE = (11.0, 15.0, 18.0, 21.0)
HALF_SENT = (26.0, 26.1, 26.2)
Y_FREE = 12.0
Z_FREE = 14.0


class Links:
    def __init__(self):
        self.free = {}

    def send(self, link, now, size):
        start = max(now, self.free.get(link, 0.0))
        self.free[link] = start + size
        return start + size + 1.0


def split(x):
    high = x.astype(BF16)
    return high, (x - high.astype(F32)).astype(BF16)


def load_tile(ref, b):
    return ref.reshape(-1, LANES, LANES)[b]


def store_tile(ref, b, value):
    ref.reshape(-1, LANES, LANES)[b] = value


def swap_low_digits(x, digit):
    rows = lax.broadcasted_iota(jnp.int32, x.shape, 0)
    lanes = lax.broadcasted_iota(jnp.int32, x.shape, 1)
    bit = 1
    while bit < digit:
        row_bit, lane_bit = rows & bit, lanes & bit
        upper = pltpu.roll(pltpu.roll(x, x.shape[0] - bit, 0), bit, 1)
        lower = pltpu.roll(pltpu.roll(x, bit, 0), x.shape[1] - bit, 1)
        x = jnp.where(row_bit == lane_bit, x, jnp.where(lane_bit == bit, upper, lower))
        bit *= 2
    return x


def kernel(
    left_count,
    right_count,
    int_hbm,
    amp_hbm,
    occ_left,
    occ_right,
    energy,
    out_hbm,
    int_own,
    amp_own,
    int_row,
    amp_row,
    int_send,
    amp_send,
    int_col,
    amp_col,
    lm,
    tl,
    lhs,
    rhs,
    acc,
    recip,
    base,
    staged,
    own_sem,
    keep_sem,
    ring_send,
    ring_recv,
    plane_send,
    plane_recv,
    lm_send,
    lm_recv,
    tl_send,
    tl_recv,
    out_sem,
):
    halves, ring = ROW_DIMS
    xs, runs, cores = COL_DIMS
    rows, cols = halves * ring, xs * runs * cores
    sub = LANES // cols
    cells = rows * sub
    r, s = lax.axis_index("row"), lax.axis_index("col")
    half, y = r // ring, r % ring
    x, run, core = s // (runs * cores), (s // cores) % runs, s % cores
    per_group = right_count // GROUPS
    group_rows = per_group * cells
    stretch = ring * sub
    per_tile = LANES // stretch
    tiles = per_group // per_tile
    amp_tiles = pl.cdiv(left_count, per_tile)

    def row_of(a, b):
        return a * ring + b

    def col_of(a, b, c):
        return (a * runs + b) * cores + c

    plane = halves * cols
    me = half * cols + s

    def in_plane(number):
        return row_of(number // cols, y), number % cols

    def remote(src, dst, send_sem, recv_sem, device):
        return pltpu.make_async_remote_copy(
            src_ref=src,
            dst_ref=dst,
            send_sem=send_sem,
            recv_sem=recv_sem,
            device_id=device,
            device_id_type=MESH,
        )

    own_copies = [
        pltpu.make_async_copy(int_hbm, int_own, own_sem.at[0]),
        pltpu.make_async_copy(amp_hbm, amp_own, own_sem.at[1]),
    ]
    for copy in own_copies:
        copy.start()

    barrier = pltpu.get_barrier_semaphore()

    def greet_ring(k, carry):
        to = row_of(half, (y + k) % ring)
        pl.semaphore_signal(barrier, inc=1, device_id=(to, s), device_id_type=MESH)
        return carry

    def greet_plane(k, carry):
        pl.semaphore_signal(barrier, inc=1, device_id=in_plane((me + k) % plane), device_id_type=MESH)
        return carry

    lax.fori_loop(1, ring, greet_ring, 0)
    lax.fori_loop(1, plane, greet_plane, 0)
    pl.semaphore_wait(barrier, ring - 1 + plane - 1)

    parts = []
    for g in range(GROUPS):
        numbers = pl.ds(g * per_group, per_group)
        parts.append((int_hbm, int_row, int_send, int_col, numbers, range(g * tiles, (g + 1) * tiles)))
    parts.append((amp_hbm, amp_row, amp_send, amp_col, pl.ds(0, left_count), range(amp_tiles)))
    for h in range(halves):
        for i in range(left_count, amp_tiles * per_tile):
            amp_row[h, i] = jnp.zeros((ring, sub, LANES), F32)

    order = list(range(GROUPS))
    order.insert(AMP_TURN, GROUPS)
    keeps = {}

    def start_ring(n):
        source, landed, _, _, numbers, _ = parts[n]

        def send_ring(k, carry):
            to = (y + k) % ring
            for h in range(halves):
                remote(
                    source.at[numbers, h, to],
                    landed.at[h, numbers, y],
                    ring_send.at[n],
                    ring_recv.at[n],
                    (row_of(half, to), s),
                ).start()
            return carry

        lax.fori_loop(1, ring, send_ring, 0)
        keeps[n] = []
        for h in range(halves):
            keep = pltpu.make_async_copy(
                source.at[numbers, h, y], landed.at[h, numbers, y], keep_sem.at[n, h]
            )
            keep.start()
            keeps[n].append(keep)

    for k, n in enumerate(order):
        if RING_SENT[k] == 0:
            start_ring(n)

    own_energy = energy[pl.ds(r, 1), :]
    lane = lax.broadcasted_iota(jnp.int32, (sub, LANES), 1)
    wanted = lax.broadcasted_iota(jnp.int32, (sub, LANES), 0) + sub * s
    for u in range(rows):
        spread = jnp.broadcast_to(energy[u : u + 1, :], (sub, LANES))
        chosen = jnp.sum(jnp.where(lane == wanted, spread, 0.0), axis=1, keepdims=True)
        base[u] = own_energy + chosen
    both_energies = base[...].reshape(cells, LANES)

    def reciprocals(j, carry):
        for i in range(left_count):
            recip[i, j] = 1.0 / (both_energies - occ_left[i] - occ_right[j])
        return carry

    lax.fori_loop(0, right_count, reciprocals, 0)

    def ring_wait(n):
        _, landed, _, _, numbers, _ = parts[n]
        whole = landed.at[:, numbers, pl.ds(0, ring - 1)]
        return remote(whole, whole, ring_send.at[n], ring_recv.at[n], (r, (s + 1) % cols))

    def plane_wait(n):
        _, _, _, arrived, _, numbers = parts[n]
        whole = arrived.at[pl.ds(numbers.start, len(numbers)), pl.ds(0, plane - 1)]
        return remote(whole, whole, plane_send.at[n], plane_recv.at[n], (r, (s + 1) % cols))

    def ring_part(n):
        _, landed, turned, arrived, _, numbers = parts[n]
        if ring > 1:
            ring_wait(n).wait_recv()
        for keep in keeps[n]:
            keep.wait()
        count = landed.shape[1] // per_tile
        for k in numbers:
            for h in range(halves):
                store_tile(turned, k * halves + h, load_tile(landed, h * count + k).T)
        slabs = pl.ds(numbers.start, len(numbers))

        def send_plane(k, carry):
            to = (me + k) % plane
            remote(
                turned.at[slabs, to],
                arrived.at[slabs, me],
                plane_send.at[n],
                plane_recv.at[n],
                in_plane(to),
            ).start()
            return carry

        lax.fori_loop(1, plane, send_plane, 0)
        for k in numbers:
            arrived[k, me] = turned[k, me]

    def plane_part(n):
        _, _, _, arrived, _, numbers = parts[n]
        plane_wait(n).wait_recv()
        for k in numbers:
            for h in range(halves):
                moved = swap_low_digits(load_tile(arrived, k * halves + h).T, sub)
                for part in range(per_tile):
                    number = k * per_tile + part
                    piece = moved[part * stretch : (part + 1) * stretch]
                    if n < GROUPS:
                        own = int_own[number, h].reshape(stretch, LANES)
                        first = number * cells + h * stretch
                        lm[r, first : first + stretch, :] = 2.0 * own - piece
                    elif number < left_count:
                        own = amp_own[number, h]
                        into = slice(h * ring, (h + 1) * ring)
                        tl[s, number, into] = 2.0 * own - piece.reshape(own.shape)

    def finish_sends(n):
        if ring > 1:
            ring_wait(n).wait_send()
        plane_wait(n).wait_send()

    sends = []
    count_of = {"lm": 0, "tl": 0}
    links = Links()
    links.free = {("y", 1): Y_FREE, ("y", -1): Y_FREE, "z": Z_FREE}
    heap = []
    serial = [0]

    def at(time, act):
        serial[0] += 1
        heapq.heappush(heap, (time, serial[0], act))

    def lm_chunk(slot, g):
        return lm.at[slot, pl.ds(g * group_rows, group_rows)]

    def send_lm(slot, g, device):
        chunk = lm_chunk(slot, g)
        copy = remote(chunk, chunk, lm_send.at[count_of["lm"]], lm_recv.at[slot, g], device)
        count_of["lm"] += 1
        copy.start()
        sends.append(copy)

    def await_lm(slot, g):
        chunk = lm_chunk(slot, g)
        remote(chunk, chunk, lm_send.at[0], lm_recv.at[slot, g], (r, (s + 1) % cols)).wait_recv()

    def send_tl(slot, device):
        chunk = tl.at[slot]
        copy = remote(chunk, chunk, tl_send.at[count_of["tl"]], tl_recv.at[slot], device)
        count_of["tl"] += 1
        copy.start()
        sends.append(copy)

    def await_tl(slot):
        chunk = tl.at[slot]
        remote(chunk, chunk, tl_send.at[0], tl_recv.at[slot], (r, (s + 1) % cols)).wait_recv()

    lm_ready, tl_ready = {}, []
    far_y, far_x = ring // 2, xs // 2
    lm_time = group_rows * LANES * 4 * 2 / 100e3
    tl_time = left_count * cells * LANES * 4 * 2 / 100e3

    def ways(distance, far, parity):
        if distance + 1 < far:
            return (1, -1)
        return ((1,) if parity else (-1,)) if distance + 1 == far else ()

    def spread_lm(now, z, g, distance, came):
        place = half if z == 0 else (half + z) % halves
        slot = row_of(place, (y - came * distance) % ring)
        if distance:
            await_lm(slot, g)
        elif z:
            await_lm(slot, g)
        lm_ready.setdefault((came * distance % ring, g), []).append(now)
        for way in ways(distance, far_y, (z + g) % 2):
            if distance == 0 or way == came:
                send_lm(slot, g, (row_of(half, (y + way) % ring), s))
                then = links.send(("y", way), now, lm_time)
                at(then, functools.partial(spread_lm, then, z, g, distance + 1, way))
        if z == 0 and distance == 0:
            later = max(now, HALF_SENT[g])
            at(later, functools.partial(cross, later, g))
        compute(now)

    def cross(now, g):
        for k in range(1, halves):
            send_lm(row_of(half, y), g, (row_of((half + k) % halves, y), s))
            then = links.send("z", now, 2 * lm_time)
            at(then, functools.partial(spread_lm, then, k, g, 0, 1))

    def spread_tl(now, k, distance, came, first):
        slot = col_of((x - came * distance) % xs, (run - k) % runs, core)
        if not first:
            await_tl(slot)
        tl_ready.append(now)
        for way in ways(distance, far_x, k % 2):
            if distance == 0 or way == came:
                send_tl(slot, (r, col_of((x + way) % xs, run, core)))
                then = links.send(("x", way), now, tl_time)
                at(then, functools.partial(spread_tl, then, k, distance + 1, way, False))
        if first:
            for other in range(1, runs):
                send_tl(slot, (r, col_of(x, (run + other) % runs, core)))
                then = links.send("z", now, tl_time)
                at(then, functools.partial(spread_tl, then, other, 0, 1, False))
        if cores > 1:
            send_tl(slot, (r, col_of(x, run, 1 - core)))
            then = links.send("core", now, tl_time / 6)
            at(then, functools.partial(sibling, then, k, distance, came))
        compute(now)

    def sibling(now, k, distance, came):
        await_tl(col_of((x - came * distance) % xs, (run - k) % runs, 1 - core))
        tl_ready.append(now)
        compute(now)

    def start_lm(now, g):
        plane_part(g)
        spread_lm(now, 0, g, 0, 1)

    def start_tl(now):
        plane_part(GROUPS)
        spread_tl(now, 0, 0, 1, True)

    prepared, done, finished = set(), set(), set()
    waiting = []

    def compute(now):
        if len(tl_ready) < cols:
            return
        if not waiting:
            waiting.append(now)
            for n, place in enumerate(nearest):
                at(now + 0.7 * n, functools.partial(prepare, now + 0.7 * n, place))
        for place in nearest:
            for g in range(GROUPS):
                ready = len(lm_ready.get((place, g), ())) == halves and place in prepared
                if ready and (place, g) not in done:
                    products(place, g, not any(other == g for _, other in done))
                    done.add((place, g))
        for g in range(GROUPS):
            if g not in finished and sum(other == g for _, other in done) == ring:
                finish(g)
                finished.add(g)

    nearest = sorted(range(ring), key=lambda place: min(place, ring - place))
    width = halves * LANES

    def prepare(now, place):
        at_y = (y - place) % ring

        def right(k, carry):
            z = k // left_count
            i = k % left_count
            high, low = split(tl[:, i, z * ring + at_y].reshape(LANES, LANES))
            across = pl.ds(pl.multiple_of(i * LANES, LANES), LANES)
            here = pl.multiple_of(z * LANES, LANES)
            rhs[at_y, pl.ds(here, LANES), across] = high
            rhs[at_y, pl.ds(width + here, LANES), across] = high
            rhs[at_y, pl.ds(2 * width + here, LANES), across] = low
            return carry

        lax.fori_loop(0, halves * left_count, right, 0)
        prepared.add(place)
        compute(now)

    def products(place, g, first):
        at_y = (y - place) % ring
        for z in range(halves):
            high, low = split(lm[row_of(z, at_y), pl.ds(g * group_rows, group_rows), :])
            lhs[:, z * LANES : (z + 1) * LANES] = high
            lhs[:, width + z * LANES : width + (z + 1) * LANES] = low
            lhs[:, 2 * width + z * LANES : 2 * width + (z + 1) * LANES] = high
        tile = 256
        here = pl.ds(g * group_rows, group_rows)

        def multiply(n, carry):
            across = pl.ds(pl.multiple_of(n * tile, tile), tile)
            product = jnp.dot(lhs[...], rhs[at_y, :, across], preferred_element_type=F32)
            acc[here, across] = product if first else acc[here, across] + product
            return carry

        lax.fori_loop(0, left_count * LANES // tile, multiply, 0)

    def finish(g):
        def scale(k, carry):
            j = g * per_group + k
            here = pl.ds(pl.multiple_of(j * cells, cells), cells)
            for i in range(left_count):
                result = acc[here, i * LANES : (i + 1) * LANES] * recip[i, j]
                staged[i, j] = result.reshape(rows, sub, LANES)
            pltpu.make_async_copy(staged.at[:, j], out_hbm.at[:, j], out_sem.at[j]).start()
            return carry

        lax.fori_loop(0, per_group, scale, 0)

    def turn(n):
        return lambda: ring_part(n)

    for k, n in enumerate(order):
        if RING_SENT[k] > 0:
            at(RING_SENT[k] + 0.01, functools.partial(start_ring, n))
        at(RING_DONE[k], turn(n))
        began = PLANE_DONE[k]
        if n < GROUPS:
            at(began, functools.partial(start_lm, began, n))
        else:
            at(began, functools.partial(start_tl, began))
    for copy in own_copies:
        at(min(PLANE_DONE) - 0.5, copy.wait)
    while heap:
        heapq.heappop(heap)[2]()
    assert len(finished) == GROUPS

    for n in range(GROUPS + 1):
        finish_sends(n)
    for copy in sends:
        copy.wait_send()

    def written(j, carry):
        pltpu.make_async_copy(staged.at[:, j], out_hbm.at[:, j], out_sem.at[j]).wait()
        return carry

    lax.fori_loop(0, right_count, written, 0)


def body(amplitudes, integrals, occupied_left, occupied_right, virtual_energy):
    left_count, rows, sub, width = amplitudes.shape
    right_count = integrals.shape[0]
    cols = width // sub
    cells = rows * sub
    halves, ring = ROW_DIMS
    per_tile = LANES // (ring * sub)
    int_tiles, amp_tiles = right_count // per_tile, pl.cdiv(left_count, per_tile)
    depth = 3 * halves * LANES
    plane = halves * cols
    dma = pltpu.SemaphoreType.DMA
    anywhere = pl.BlockSpec(memory_space=pl.ANY)
    scalars = pl.BlockSpec(memory_space=pltpu.SMEM)
    return pl.pallas_call(
        functools.partial(kernel, left_count, right_count),
        out_shape=jax.ShapeDtypeStruct((left_count, right_count, rows, sub, width), F32),
        in_specs=[
            anywhere,
            anywhere,
            scalars,
            scalars,
            pl.BlockSpec(memory_space=pltpu.VMEM),
        ],
        out_specs=anywhere,
        scratch_shapes=[
            pltpu.VMEM((right_count, halves, ring, sub, LANES), F32),
            pltpu.VMEM((left_count, halves, ring, sub, LANES), F32),
            pltpu.VMEM((halves, right_count, ring, sub, LANES), F32),
            pltpu.VMEM((halves, amp_tiles * per_tile, ring, sub, LANES), F32),
            pltpu.VMEM((int_tiles, plane, sub, LANES), F32),
            pltpu.VMEM((amp_tiles, plane, sub, LANES), F32),
            pltpu.VMEM((int_tiles, plane, sub, LANES), F32),
            pltpu.VMEM((amp_tiles, plane, sub, LANES), F32),
            pltpu.VMEM((rows, right_count * cells, LANES), F32),
            pltpu.VMEM((cols,) + amplitudes.shape, F32),
            pltpu.VMEM((right_count // GROUPS * cells, depth), BF16),
            pltpu.VMEM((ROW_DIMS[1], depth, left_count * LANES), BF16),
            pltpu.VMEM((right_count * cells, left_count * LANES), F32),
            pltpu.VMEM((left_count, right_count, cells, LANES), F32),
            pltpu.VMEM((rows, sub, LANES), F32),
            pltpu.VMEM((left_count, right_count, rows, sub, LANES), F32),
            dma((2,)),
            dma((GROUPS + 1, halves)),
            dma((GROUPS + 1,)),
            dma((GROUPS + 1,)),
            dma((GROUPS + 1,)),
            dma((GROUPS + 1,)),
            dma((16 * GROUPS,)),
            dma((rows, GROUPS)),
            dma((40,)),
            dma((cols,)),
            dma((right_count,)),
        ],
        compiler_params=pltpu.CompilerParams(
            collective_id=0, has_side_effects=True, vmem_limit_bytes=60 * 1024 * 1024
        ),
    )(
        integrals.reshape(right_count, halves, ring, sub, width),
        amplitudes.reshape(left_count, halves, ring, sub, width),
        occupied_left,
        occupied_right,
        virtual_energy.reshape(rows, width),
    )


def solution(mesh):
    return jax.shard_map(
        body,
        mesh=mesh,
        in_specs=(P(None, None, "col", "row"), P(None, None, "col", "row"), P(), P(), P()),
        out_specs=P(None, None, None, "col", "row"),
        check_vma=False,
    )
```

time: 143 us -> 125 us (0.87)
  the two profiles are of different devices: /device:TPU:177 before, /device:TPU:64 now
where the time goes in v2:
time: 125 us
  Pallas kernels  122 us (98%)
  local copies, waits for them, and re-layouts  3.36 us (3%)
    pallas_call x1, Pallas kernels, body(): pl.pallas_call(functools.partial(kernel, left_count, right_count), out_sh...  122 us
    unnamed x1, local copies, waits for them, and re-layouts  3.36 us

profile of v2, /device:TPU:64, one launch (start us, length us, event | category | flops | bytes accessed | tf_op | source)
XLA Modules:
  0.0 125.0 jit_solution(763544598715846597)
XLA Ops:
  0.0 121.6 %shard_map.55 = f32[6,12,16,4,128]{4,3,2,1,0:T(4,128)} custom-call(f32[12,2,8,4,128]{4,3,2,1,0:T(4,128)} %bitcast.3, f32[6,2,8,4,128]{4,3,2,1,0:T(4,128)} %bitcast.4, f32[6]{0:T(128)} %occ_left.1, f32[12]{0:T(128)} %occ_right.1, f32[16,128]{1,0:T(8,128)} %bitcast.5), custom_call_target="tpu_custom_call" | custom-call | tf_op jit(solution)/shard_map/pallas_call | solution.py:496
  121.6 3.4 %copy.7 = f32[6,12,16,4,128]{4,3,2,1,0:T(4,128)} copy(f32[6,12,16,4,128]{4,3,2,1,0:T(4,128)} %shard_map.55) | data formatting | bytes 4718592

commit v3 on v2

--- a/solution.py
+++ b/solution.py
@@ -20,7 +20,8 @@
 RING_SENT = (0.0, 0.0, 0.0, 0.0)
 RING_DONE = (4.5, 7.0, 9.5, 12.5)
 PLANE_DONE = (11.0, 15.0, 18.0, 21.0)
-HALF_SENT = (26.0, 26.1, 26.2)
+HALF_SENT = (0.0, 0.0, 0.0)
+RUN_SENT = (26.5, 26.5, 26.5)
 Y_FREE = 12.0
 Z_FREE = 14.0
 
@@ -356,14 +357,18 @@
                 at(then, functools.partial(spread_tl, then, k, distance + 1, way, False))
         if first:
             for other in range(1, runs):
-                send_tl(slot, (r, col_of(x, (run + other) % runs, core)))
-                then = links.send("z", now, tl_time)
-                at(then, functools.partial(spread_tl, then, other, 0, 1, False))
+                later = max(now, RUN_SENT[other - 1])
+                at(later, functools.partial(along, later, other))
         if cores > 1:
             send_tl(slot, (r, col_of(x, run, 1 - core)))
             then = links.send("core", now, tl_time / 6)
             at(then, functools.partial(sibling, then, k, distance, came))
         compute(now)
+
+    def along(now, other):
+        send_tl(col_of(x, run, core), (r, col_of(x, (run + other) % runs, core)))
+        then = links.send("z", now, tl_time)
+        at(then, functools.partial(spread_tl, then, other, 0, 1, False))
 
     def sibling(now, k, distance, came):
         await_tl(col_of((x - came * distance) % xs, (run - k) % runs, 1 - core))

time: 125 us -> 132 us (1.056)
  the two profiles are of different devices: /device:TPU:64 before, /device:TPU:1 now
where the time goes in v3:
time: 132 us
  Pallas kernels  128 us (97%)
  local copies, waits for them, and re-layouts  3.36 us (3%)
    pallas_call x1, Pallas kernels, body(): pl.pallas_call(functools.partial(kernel, left_count, right_count), out_sh...  128 us
    unnamed x1, local copies, waits for them, and re-layouts  3.36 us

profile of v3, /device:TPU:1, one launch (start us, length us, event | category | flops | bytes accessed | tf_op | source)
XLA Modules:
  0.0 131.8 jit_solution(16740241668319675359)
XLA Ops:
  0.0 128.4 %shard_map.55 = f32[6,12,16,4,128]{4,3,2,1,0:T(4,128)} custom-call(f32[12,2,8,4,128]{4,3,2,1,0:T(4,128)} %bitcast.3, f32[6,2,8,4,128]{4,3,2,1,0:T(4,128)} %bitcast.4, f32[6]{0:T(128)} %occ_left.1, f32[12]{0:T(128)} %occ_right.1, f32[16,128]{1,0:T(8,128)} %bitcast.5), custom_call_target="tpu_custom_call" | custom-call | tf_op jit(solution)/shard_map/pallas_call | solution.py:501
  128.4 3.4 %copy.7 = f32[6,12,16,4,128]{4,3,2,1,0:T(4,128)} copy(f32[6,12,16,4,128]{4,3,2,1,0:T(4,128)} %shard_map.55) | data formatting | bytes 4718592

commit v4 on v3

--- a/solution.py
+++ b/solution.py
@@ -21,7 +21,7 @@
 RING_DONE = (4.5, 7.0, 9.5, 12.5)
 PLANE_DONE = (11.0, 15.0, 18.0, 21.0)
 HALF_SENT = (0.0, 0.0, 0.0)
-RUN_SENT = (26.5, 26.5, 26.5)
+RUN_SENT = (0.0, 26.5, 26.5)
 Y_FREE = 12.0
 Z_FREE = 14.0
 

time: 132 us -> 123 us (0.932)
  Pallas kernels: 128 us -> 120 us
    pallas_call x1, Pallas kernels: 128 us -> 120 us  [body(): pl.pallas_call(functools.partial(kernel, left_count, right_count), out_sh...]
where the time goes in v4:
time: 123 us
  Pallas kernels  120 us (98%)
  local copies, waits for them, and re-layouts  3.36 us (3%)
    pallas_call x1, Pallas kernels, body(): pl.pallas_call(functools.partial(kernel, left_count, right_count), out_sh...  120 us
    unnamed x1, local copies, waits for them, and re-layouts  3.36 us

profile of v4, /device:TPU:1, one launch (start us, length us, event | category | flops | bytes accessed | tf_op | source)
XLA Modules:
  0.0 123.1 jit_solution(9932016093957160333)
XLA Ops:
  0.0 119.7 %shard_map.55 = f32[6,12,16,4,128]{4,3,2,1,0:T(4,128)} custom-call(f32[12,2,8,4,128]{4,3,2,1,0:T(4,128)} %bitcast.3, f32[6,2,8,4,128]{4,3,2,1,0:T(4,128)} %bitcast.4, f32[6]{0:T(128)} %occ_left.1, f32[12]{0:T(128)} %occ_right.1, f32[16,128]{1,0:T(8,128)} %bitcast.5), custom_call_target="tpu_custom_call" | custom-call | tf_op jit(solution)/shard_map/pallas_call | solution.py:501
  119.7 3.4 %copy.7 = f32[6,12,16,4,128]{4,3,2,1,0:T(4,128)} copy(f32[6,12,16,4,128]{4,3,2,1,0:T(4,128)} %shard_map.55) | data formatting | bytes 4718592
